TPU v7x, 32 devices: a whole 2x2x4 slice. The times are simulated.
32 devices in a mesh: dp: 4 (over y, x), tensor: 8 (over z, core).
Axes of the slice: x: 2, y: 2, z: 4, core: 2. Of those that a mesh axis runs over, the one named last changes fastest.
Arguments:
- tokens_in: bfloat16 [2048, 128, 128], P('dp', 'tensor'), may hold values from -6 to 6
- right_one: bfloat16 [128, 128, 128], P('tensor'), may hold values from -0.5 to 0.5
- left_one: bfloat16 [128, 128, 128], P('tensor'), may hold values from -0.5 to 0.5
- right_two: bfloat16 [128, 128, 128], P('tensor'), may hold values from -0.5 to 0.5
- left_two: bfloat16 [128, 128, 128], P('tensor'), may hold values from -0.5 to 0.5
- out_grad: bfloat16 [2048, 128, 128], P('dp', 'tensor'), may hold values from -6 to 6
Outputs:
- layer_out: bfloat16 [2048, 128, 128], P('dp', 'tensor')
- input_grad: bfloat16 [2048, 128, 128], P('dp', 'tensor')
- grad_right_one: float32 [128, 128, 128], P('tensor', 'dp')
- grad_left_one: float32 [128, 128, 128], P('tensor', 'dp')
- grad_right_two: float32 [128, 128, 128], P('tensor', 'dp')
- grad_left_two: float32 [128, 128, 128], P('tensor', 'dp')
All inputs are finite; a program needn't handle non-finite values.
Results may differ from a plain program's by a relative error of at most 0.0067.
Values may be sent and summed in bfloat16 or wider, within the bound.
A program may use at most 64 MiB of HBM per device.

v0:
```python
import math

import jax
import jax.numpy as jnp
from jax import lax
from jax.sharding import PartitionSpec as P


def gelu_value(z):
    return 0.5 * z * (1.0 + lax.erf(z / math.sqrt(2.0)))


def gelu_slope(z):
    return 0.5 * (1.0 + lax.erf(z / math.sqrt(2.0))) + z * jnp.exp(-0.5 * z * z) / math.sqrt(
        2.0 * math.pi
    )


def gather_factor(factor, n_dp):
    blocks, rows, cols = factor.shape
    flat = factor.reshape(blocks * rows, cols)
    part = flat.shape[0] // n_dp
    mine = lax.dynamic_slice_in_dim(flat, lax.axis_index("dp") * part, part, axis=0)
    whole = lax.all_gather(mine, ("tensor", "dp"), axis=0, tiled=True)
    return whole.reshape(-1, rows, cols)


def reduce_all(grad):
    grad = lax.psum_scatter(grad.astype(jnp.bfloat16), "dp", scatter_dimension=1, tiled=True)
    return lax.psum_scatter(grad, "tensor", scatter_dimension=0, tiled=True).astype(jnp.float32)


def to_tokens(values):
    return lax.all_to_all(values, "tensor", split_axis=0, concat_axis=1, tiled=True)


def to_blocks(values):
    return lax.all_to_all(values, "tensor", split_axis=1, concat_axis=0, tiled=True)


def make(n_dp):
    def on_device(tokens_in, right_one, left_one, right_two, left_two, out_grad):
        bf = jnp.bfloat16
        f32 = jnp.float32

        def dot(spec, a, b):
            return jnp.einsum(spec, a, b, preferred_element_type=f32)

        u1 = dot("tbi,bio->tbo", tokens_in, right_one).astype(bf)
        v1 = to_tokens(u1)
        left_one = gather_factor(left_one, n_dp)
        right_two = gather_factor(right_two, n_dp)
        left_two = gather_factor(left_two, n_dp)
        dw_two = to_tokens(out_grad)
        z1 = dot("tbj,jbk->tjk", v1, left_one).astype(bf)
        hidden = gelu_value(z1.astype(f32)).astype(bf)
        u2 = dot("tjk,kjm->tkm", hidden, right_two).astype(bf)
        w2 = dot("tkm,mkn->tnm", u2, left_two).astype(bf)
        mixed = to_blocks(w2)
        layer_out = (tokens_in.astype(f32) + mixed.astype(f32)).astype(bf)
        du2 = dot("tnm,mkn->tkm", dw_two, left_two).astype(bf)
        gl2 = reduce_all(dot("tkm,tnm->mkn", u2, dw_two))
        gr2 = reduce_all(dot("tjk,tkm->kjm", hidden, du2))
        dh = dot("tkm,kjm->tjk", du2, right_two)
        dz1 = (dh * gelu_slope(z1.astype(f32))).astype(bf)
        dv1 = dot("tjk,jbk->tbj", dz1, left_one).astype(bf)
        du1 = to_blocks(dv1)
        gl1 = reduce_all(dot("tbj,tjk->jbk", v1, dz1))
        gr1 = dot("tbi,tbo->bio", tokens_in, du1)
        input_grad = (out_grad.astype(f32) + dot("tbo,bio->tbi", du1, right_one)).astype(bf)
        gr1 = lax.psum_scatter(gr1, "dp", scatter_dimension=1, tiled=True)
        return (layer_out, input_grad, gr1, gl1, gr2, gl2)

    return on_device


def solution(mesh):
    split = P("dp", "tensor", None)
    factor = P("tensor", None, None)
    grad = P("tensor", "dp", None)
    return jax.shard_map(
        make(mesh.shape["dp"]),
        mesh=mesh,
        in_specs=(split, factor, factor, factor, factor, split),
        out_specs=(split, split, grad, grad, grad, grad),
        check_vma=False,
    )
```

profile of v0, /device:TPU:8, one launch (start us, length us, event | category | flops | bytes accessed | tf_op | source)
XLA Modules:
  0.0 564.8 jit_solution(3764262376129651941)
XLA Ops:
  10.5 5.5 all-to-all-start.2
  24.8 45.3 %all-to-all-done.2 = bf16[512,16,128]{2,1,0:T(8,128)(2,1)} async-done(((bf16[512,16,128]{2,1,0:T(8,128)(2,1)}), bf16[512,16,128]{2,1,0:T(8,128)(2,1)}, u32[]{:S(2)}, u32[]{:S(2)}) %all-to-all-start.2) | async-done | bytes 2097184 | tf_op jit(solution)/shard_map/all_to_all | solution.py:34
  70.0 7.9 %all-to-all-start = ((bf16[512,16,128]{2,1,0:T(8,128)(2,1)}), bf16[512,16,128]{2,1,0:T(8,128)(2,1)}, u32[]{:S(2)}, u32[]{:S(2)}) async-start(bf16[512,16,128]{2,1,0:T(8,128)(2,1)} %copy.108), calls=%async_computation | async-start | bytes 4194304 | tf_op jit(solution)/shard_map/all_to_all | solution.py:34
  84.7 46.3 %all-to-all-done = bf16[512,16,128]{2,1,0:T(8,128)(2,1)} async-done(((bf16[512,16,128]{2,1,0:T(8,128)(2,1)}), bf16[512,16,128]{2,1,0:T(8,128)(2,1)}, u32[]{:S(2)}, u32[]{:S(2)}) %all-to-all-start) | async-done | bytes 2097184 | tf_op jit(solution)/shard_map/all_to_all | solution.py:34
  138.7 6.5 %convolution_convert_fusion.4 = bf16[128,128,64]{1,2,0:T(8,128)(2,1)} fusion(bf16[128,128,128]{2,1,0:T(8,128)(2,1)} %bitcast.82, bf16[64,128,128]{1,0,2:T(8,128)(2,1)S(1)} %copy.118), kind=kOutput, calls=%fused_computation.26 | convolution fusion | flops 269484032 | bytes 8388608 | tf_op jit(solution)/shard_map/tnm,mkn->tkm/dot_general | solution.py:47
  149.0 26.1 %all-gather.6.cloned.1.call-done = bf16[16384,128]{1,0:T(8,128)(2,1)} async-done(((bf16[512,128]{1,0:T(8,128)(2,1)}), bf16[16384,128]{1,0:T(8,128)(2,1)}) %all-gather.6.cloned.1.call-update) | async-done | bytes 4194320 | tf_op jit(solution)/shard_map/all_gather | solution.py:24
  175.0 7.1 %fusion.18 = f32[128,128,64]{1,2,0:T(8,128)} fusion(bf16[128,128,128]{2,1,0:T(8,128)(2,1)} %bitcast.84, bf16[128,128,64]{0,2,1:T(8,128)(2,1)S(1)} %copy.119), kind=kOutput, calls=%fused_computation.34 | convolution fusion | flops 268435456 | bytes 10485760 | tf_op jit(solution)/shard_map/tkm,kjm->tjk/dot_general | solution.py:47
  182.1 5.5 copy.120
  187.6 51.5 %all-gather.8.cloned.1.call-done = bf16[16384,128]{1,0:T(8,128)(2,1)} async-done(((bf16[512,128]{1,0:T(8,128)(2,1)}), bf16[16384,128]{1,0:T(8,128)(2,1)}) %all-gather.8.cloned.1.call-update) | async-done | bytes 4194320 | tf_op jit(solution)/shard_map/all_gather | solution.py:24
  239.1 7.1 %fusion.5 = (bf16[64,128,128]{2,0,1:T(8,128)(2,1)}, bf16[64,128,128]{2,0,1:T(8,128)(2,1)}) fusion(f32[128,128,64]{0,2,1:T(8,128)} %copy.120, bf16[64,128,128]{1,0,2:T(8,128)(2,1)} %copy.110, bf16[128,128,128]{2,1,0:T(8,128)(2,1)} %bitcast.90), kind=kOutput, calls=%fused_computation.6 | convolution fusion | flops 284164096 | bytes 14680064 | tf_op jit(solution)/shard_map/tbj,jbk->tjk/dot_general | solution.py:47
  250.8 5.4 convert_bitcast_fusion.3
  260.8 5.5 convolution_convert_fusion
  266.5 4.9 convolution_convert_fusion.1
  273.4 4.9 convolution_convert_fusion.2
  279.9 6.8 %convert_bitcast_fusion.1 = bf16[64,128,128]{1,0,2:T(8,128)(2,1)} fusion(bf16[128,128,128]{2,1,0:T(8,128)(2,1)} %bitcast.91, bf16[64,128,128]{2,0,1:T(8,128)(2,1)S(1)} %copy-done.6), kind=kOutput, calls=%fused_computation.21 | convolution fusion | flops 269484032 | bytes 8388608 | tf_op jit(solution)/shard_map/tjk,jbk->tbj/dot_general | solution.py:47
  290.5 50.1 %all_to_all.63 = bf16[64,128,128]{2,0,1:T(8,128)(2,1)S(1)} all-to-all(bf16[64,128,128]{2,0,1:T(8,128)(2,1)S(1)} %copy.121), channel_id=1, replica_groups=mesh['dp'=4,'tensor'=8] {'tensor'}, dimensions={1} | all-to-all | bytes 4194304 | tf_op jit(solution)/shard_map/all_to_all | solution.py:38
  348.1 5.4 convert_bitcast_fusion.2
  358.0 6.6 %all-to-all-start.1 = ((bf16[64,128,128]{2,0,1:T(8,128)(2,1)}), bf16[64,128,128]{2,0,1:T(8,128)(2,1)}, u32[]{:S(2)}, u32[]{:S(2)}) async-start(bf16[64,128,128]{2,0,1:T(8,128)(2,1)} %copy.113), calls=%async_computation.1 | async-start | bytes 4194304 | tf_op jit(solution)/shard_map/all_to_all | solution.py:38
  364.6 8.8 %reduce-scatter.14.cloned.1.call-done = bf16[128,32,128]{2,1,0:T(8,128)(2,1)} async-done(((bf16[128,128,128]{2,1,0:T(8,128)(2,1)}), bf16[128,32,128]{2,1,0:T(8,128)(2,1)}) %reduce-scatter.14.cloned.1.call-update) | async-done | bytes 1048592 | tf_op jit(solution)/shard_map/reduce_scatter | solution.py:29
  373.8 55.2 %reduce-scatter.10.cloned.1.call-done = bf16[128,32,128]{2,1,0:T(8,128)(2,1)} async-done(((bf16[128,128,128]{2,1,0:T(8,128)(2,1)}), bf16[128,32,128]{2,1,0:T(8,128)(2,1)}) %reduce-scatter.10.cloned.1.call-update) | async-done | bytes 1048592 | tf_op jit(solution)/shard_map/reduce_scatter | solution.py:29
  440.9 18.9 %reduce-scatter.8.cloned.1.call-done = f32[16,32,128]{2,0,1:T(8,128)} async-done(((f32[16,128,128]{2,0,1:T(8,128)}), f32[16,32,128]{2,0,1:T(8,128)}) %reduce-scatter.8.cloned.1.call-update) | async-done | bytes 262160 | tf_op jit(solution)/shard_map/reduce_scatter | solution.py:71
  461.6 29.1 %reduce-scatter.20.cloned.1.call-done = bf16[16,32,128]{2,1,0:T(8,128)(2,1)} async-done(((bf16[128,32,128]{2,1,0:T(8,128)(2,1)}), bf16[16,32,128]{2,1,0:T(8,128)(2,1)}) %reduce-scatter.20.cloned.1.call-update) | async-done | bytes 131088 | tf_op jit(solution)/shard_map/reduce_scatter | solution.py:30
  492.3 31.3 %reduce-scatter.16.cloned.1.call-done = bf16[16,32,128]{2,1,0:T(8,128)(2,1)} async-done(((bf16[128,32,128]{2,1,0:T(8,128)(2,1)}), bf16[16,32,128]{2,1,0:T(8,128)(2,1)}) %reduce-scatter.16.cloned.1.call-update) | async-done | bytes 131088 | tf_op jit(solution)/shard_map/reduce_scatter | solution.py:30
  525.2 31.1 %reduce-scatter.12.cloned.1.call-done = bf16[16,32,128]{2,1,0:T(8,128)(2,1)} async-done(((bf16[128,32,128]{2,1,0:T(8,128)(2,1)}), bf16[16,32,128]{2,1,0:T(8,128)(2,1)}) %reduce-scatter.12.cloned.1.call-update) | async-done | bytes 131088 | tf_op jit(solution)/shard_map/reduce_scatter | solution.py:30
  (64 shorter events, 77.9 us)
Async XLA Ops:
  7.2 10.4 %copy-start = (bf16[16,128,128]{2,1,0:T(8,128)(2,1)S(1)}, bf16[16,128,128]{2,1,0:T(8,128)(2,1)}, u32[]{:S(2)}) copy-start(bf16[16,128,128]{2,1,0:T(8,128)(2,1)} %param.7) | copy-start | bytes 1572868
  7.2 131.5 %all-gather.4.cloned.1.call-start = ((), (), s32[]{:S(2)}) async-start(), calls=%async_computation.11 | async-start | bytes 4325376 | tf_op jit(solution)/shard_map/all_gather | solution.py:24
  8.9 166.2 %all-gather.6.cloned.1.call-start = ((), (), s32[]{:S(2)}) async-start(), calls=%async_computation.12 | async-start | bytes 4325376 | tf_op jit(solution)/shard_map/all_gather | solution.py:24
  10.5 7.1 %copy-start.1 = (bf16[512,16,128]{2,1,0:T(8,128)(2,1)S(1)}, bf16[512,16,128]{2,1,0:T(8,128)(2,1)}, u32[]{:S(2)}) copy-start(bf16[512,16,128]{2,1,0:T(8,128)(2,1)} %param.6) | copy-start | bytes 6291460
  10.5 59.5 %all-to-all-start.2 = ((bf16[512,16,128]{2,1,0:T(8,128)(2,1)}), bf16[512,16,128]{2,1,0:T(8,128)(2,1)}, u32[]{:S(2)}, u32[]{:S(2)}) async-start(bf16[512,16,128]{2,1,0:T(8,128)(2,1)} %param.11), calls=%async_computation.2 | async-start | bytes 4194304 | tf_op jit(solution)/shard_map/all_to_all | solution.py:34
  16.0 223.1 %all-gather.8.cloned.1.call-start = ((), (), s32[]{:S(2)}) async-start(), calls=%async_computation.13 | async-start | bytes 4325376 | tf_op jit(solution)/shard_map/all_gather | solution.py:24
  70.0 61.0 %all-to-all-start = ((bf16[512,16,128]{2,1,0:T(8,128)(2,1)}), bf16[512,16,128]{2,1,0:T(8,128)(2,1)}, u32[]{:S(2)}, u32[]{:S(2)}) async-start(bf16[512,16,128]{2,1,0:T(8,128)(2,1)} %copy.108), calls=%async_computation | async-start | bytes 4194304 | tf_op jit(solution)/shard_map/all_to_all | solution.py:34
  77.9 269.5 %reduce-scatter.18.cloned.1.call-start = ((), (), s32[]{:S(2)}) async-start(), calls=%async_computation.19 | async-start | bytes 5242880 | tf_op jit(solution)/shard_map/reduce_scatter | solution.py:29
  84.7 53.9 %copy-start.4 = (bf16[64,128,128]{1,0,2:T(8,128)(2,1)}, bf16[64,128,128]{1,0,2:T(8,128)(2,1)S(1)}, u32[]{:S(2)}) copy-start(bf16[64,128,128]{1,0,2:T(8,128)(2,1)S(1)} %copy.118) | copy-start | bytes 6291460
  266.3 107.2 %reduce-scatter.14.cloned.1.call-start = ((), (), s32[]{:S(2)}) async-start(), calls=%async_computation.17 | async-start | bytes 5242880 | tf_op jit(solution)/shard_map/reduce_scatter | solution.py:29
  271.4 2.0 copy-start.5
  271.5 157.5 %reduce-scatter.10.cloned.1.call-start = ((), (), s32[]{:S(2)}) async-start(), calls=%async_computation.15 | async-start | bytes 5242880 | tf_op jit(solution)/shard_map/reduce_scatter | solution.py:29
  278.3 1.6 copy-start.6
  278.3 181.5 %reduce-scatter.8.cloned.1.call-start = ((), (), s32[]{:S(2)}) async-start(), calls=%async_computation.14 | async-start | bytes 1310720 | tf_op jit(solution)/shard_map/reduce_scatter | solution.py:71
  340.6 1.6 copy-start.2
  347.3 143.4 %reduce-scatter.20.cloned.1.call-start = ((), (), s32[]{:S(2)}) async-start(), calls=%async_computation.20 | async-start | bytes 1179648 | tf_op jit(solution)/shard_map/reduce_scatter | solution.py:30
  358.0 76.1 %all-to-all-start.1 = ((bf16[64,128,128]{2,0,1:T(8,128)(2,1)}), bf16[64,128,128]{2,0,1:T(8,128)(2,1)}, u32[]{:S(2)}, u32[]{:S(2)}) async-start(bf16[64,128,128]{2,0,1:T(8,128)(2,1)} %copy.113), calls=%async_computation.1 | async-start | bytes 4194304 | tf_op jit(solution)/shard_map/all_to_all | solution.py:38
  364.6 159.0 %reduce-scatter.16.cloned.1.call-start = ((), (), s32[]{:S(2)}) async-start(), calls=%async_computation.18 | async-start | bytes 1179648 | tf_op jit(solution)/shard_map/reduce_scatter | solution.py:30
  373.5 182.9 %reduce-scatter.12.cloned.1.call-start = ((), (), s32[]{:S(2)}) async-start(), calls=%async_computation.16 | async-start | bytes 1179648 | tf_op jit(solution)/shard_map/reduce_scatter | solution.py:30
  437.5 1.6 copy-start.3
Sparse Core Ops, SparseCore 0:
  11.5 82.3 all-gather.3
  97.3 77.7 all-gather.5
  178.5 60.5 all-gather.7
  266.4 51.2 reduce-scatter.17
  320.8 52.6 reduce-scatter.13
  376.3 52.6 reduce-scatter.9
  432.1 27.6 reduce-scatter.7
  462.1 28.5 reduce-scatter.19
  493.0 30.5 reduce-scatter.15
  525.7 30.5 reduce-scatter.11
where the time goes:
time: 572 us; the launch traced here: 565 us
  waiting for transfers between devices  344 us (60%)
  local copies, waits for them, and re-layouts  67.1 us (12%)
  matrix products  60.9 us (11%)
  blocking collectives  50.1 us (9%)
  starting transfers between devices  20.8 us (4%)
  between operations  14.3 us (2%)
  other arithmetic  7.17 us (1%)
    all_to_all x2, waiting for transfers between devices, to_tokens(): lax.all_to_all(values, 'tensor', split_axis=0, concat_axis=1, tiled=True)  91.6 us
    reduce_scatter x3, waiting for transfers between devices, reduce_all(): lax.psum_scatter(grad, 'tensor', scatter_dimension=0, tiled=True)  91.5 us
    all_gather x3, waiting for transfers between devices, gather_factor(): whole = lax.all_gather(mine, ('tensor', 'dp'), axis=0, tiled=True)  77.6 us
    reduce_scatter x3, waiting for transfers between devices, reduce_all(): lax.psum_scatter(grad.astype(jnp.bfloat16), 'dp', scatter_dimension=1, ti...  64 us
    dot_general x12, matrix products, dot(): return jnp.einsum(spec, a, b, preferred_element_type=f32)  60.9 us
    all_to_all x1, blocking collectives, to_blocks(): lax.all_to_all(values, 'tensor', split_axis=1, concat_axis=0, tiled=True)  50.1 us
    reduce_scatter x1, waiting for transfers between devices, on_device(): gr1 = lax.psum_scatter(gr1, 'dp', scatter_dimension=1, tiled=True)  18.9 us
    all_to_all x4, local copies, waits for them, and re-layouts, to_tokens(): lax.all_to_all(values, 'tensor', split_axis=0, concat_axis=1, tiled=True)  14.4 us
  transfers between devices with their start and end apart: 13, of which 10 were waited for; matrix products, arithmetic and copies ran while one was open for 17% of the time, Pallas kernels for 0%

commit v1 on v0

v1 whole, which is shorter than its diff:
```python
import math

import jax
import jax.numpy as jnp
from jax import lax
from jax.experimental import pallas as pl
from jax.experimental.pallas import tpu as pltpu
from jax.sharding import PartitionSpec as P


def gelu_value(z):
    return 0.5 * z * (1.0 + lax.erf(z / math.sqrt(2.0)))


def gelu_slope(z):
    return 0.5 * (1.0 + lax.erf(z / math.sqrt(2.0))) + z * jnp.exp(-0.5 * z * z) / math.sqrt(
        2.0 * math.pi
    )


MESH = pl.DeviceIdType.MESH


def place():
    rank = lax.axis_index("tensor")
    return lax.axis_index("dp"), lax.div(rank, 2), lax.rem(rank, 2)


def greet(peers):
    barrier = pltpu.get_barrier_semaphore()
    for peer in peers:
        pl.semaphore_signal(barrier, inc=1, device_id=peer, device_id_type=MESH)
    pl.semaphore_wait(barrier, len(peers))


def peers_of(n_dp, n_z):
    d, z, c = place()
    along_z = [(d, lax.rem(z + k, n_z) * 2 + c) for k in range(1, n_z)]
    along_dp = [(lax.rem(d + k, n_dp), z * 2 + c) for k in range(1, n_dp)]
    return along_z, along_dp, (d, z * 2 + 1 - c)


def remote(src, dst, send, recv, peer):
    return pltpu.make_async_remote_copy(
        src_ref=src, dst_ref=dst, send_sem=send, recv_sem=recv, device_id=peer, device_id_type=MESH
    )


def gather_kernel(n_dp, n_z, count, *refs):
    shards, (sent, wholes), sems = refs[:count], (refs[count], refs[count + 1 : 2 * count + 1]), refs[2 * count + 1 :]
    got = sems[0]
    own_sem, zs, zr, ds, dr, cs, cr, us, ur, ul = sems[1:]
    d, z, c = place()
    n = n_z * 2
    rank = z * 2 + c
    along_z, along_dp, sibling = peers_of(n_dp, n_z)
    others = [lax.rem(rank + k, n) for k in range(1, n)]
    greet([(d, p) for p in others] + along_dp)
    swaps = [remote(sent.at[p], got.at[rank], us.at[i], ur.at[i], (d, p)) for i, p in enumerate(others)]
    keep = pltpu.make_async_copy(sent.at[rank], got.at[rank], ul)
    stage_z, own = [], []
    for f in range(count):
        own.append(pltpu.make_async_copy(shards[f].at[d], wholes[f].at[z, c, d], own_sem.at[f]))
        stage_z.append([
            remote(shards[f].at[d], wholes[f].at[z, c, d], zs.at[f, i], zr.at[f, i], p)
            for i, p in enumerate(along_z)
        ])
    for f in range(count):
        own[f].start()
        for copy in stage_z[f]:
            copy.start()
    stage_dp = []
    for f in range(count):
        own[f].wait()
        for copy in stage_z[f]:
            copy.wait()
        part = wholes[f].at[:, c, d]
        stage_dp.append([remote(part, part, ds.at[f, i], dr.at[f, i], p) for i, p in enumerate(along_dp)])
        for copy in stage_dp[f]:
            copy.start()
    keep.start()
    for copy in swaps:
        copy.start()
    stage_core = []
    for f in range(count):
        for copy in stage_dp[f]:
            copy.wait()
        half = wholes[f].at[:, c]
        stage_core.append(remote(half, half, cs.at[f], cr.at[f], sibling))
        stage_core[f].start()
    for copy in stage_core:
        copy.wait()
    keep.wait()
    for copy in swaps:
        copy.wait()


def gather_and_swap(values, factors, n_dp, n_z):
    count, n = len(factors), n_z * 2
    blocks, rows, cols = factors[0].shape
    part = blocks * rows // n_dp
    shards = [f.reshape(n_dp, part, cols) for f in factors]
    sent = values.reshape((n, values.shape[0] // n) + values.shape[1:])
    dma = pltpu.SemaphoreType.DMA
    hbm = pl.BlockSpec(memory_space=pl.ANY)
    out = pl.pallas_call(
        lambda *refs: gather_kernel(n_dp, n_z, count, *refs),
        out_shape=[jax.ShapeDtypeStruct((n_z, 2, n_dp, part, cols), f.dtype) for f in factors]
        + [jax.ShapeDtypeStruct(sent.shape, sent.dtype)],
        in_specs=[hbm] * (count + 1),
        out_specs=[hbm] * (count + 1),
        scratch_shapes=[
            dma((count,)),
            dma((count, n_z - 1)),
            dma((count, n_z - 1)),
            dma((count, n_dp - 1)),
            dma((count, n_dp - 1)),
            dma((count,)),
            dma((count,)),
            dma((n - 1,)),
            dma((n - 1,)),
            dma,
        ],
        compiler_params=pltpu.CompilerParams(collective_id=0, has_side_effects=True),
        cost_estimate=pl.CostEstimate(flops=0, bytes_accessed=64 * 2**20, transcendentals=0),
    )(*shards, sent)
    return [w.reshape(n * blocks, rows, cols) for w in out[:count]], out[count]


def reduce_kernel(n_dp, n_z, count, *refs):
    f32, bf = jnp.float32, jnp.bfloat16
    grads, outs, rest = refs[:count], refs[count : 2 * count], refs[2 * count :]
    own, got_c, sum_c, got_d, sum_d, got_z, own_sem, cs, cr, ds, dr, zs, zr = rest
    d, z, c = place()
    along_z, along_dp, sibling = peers_of(n_dp, n_z)
    greet(along_z + along_dp + [sibling])
    stage_c, local = [], []
    for f in range(count):
        stage_c.append(remote(grads[f].at[:, 1 - c], got_c.at[f], cs.at[f], cr.at[f], sibling))
        local.append(pltpu.make_async_copy(grads[f].at[:, c], own.at[f], own_sem.at[f]))
        stage_c[f].start()
        local[f].start()
    stage_d = []
    for f in range(count):
        stage_c[f].wait()
        local[f].wait()

        def core_sum(k, carry):
            for q in range(n_dp):
                total = own[f, k, :, q].astype(f32) + got_c[f, k, :, q].astype(f32)
                sum_c[f, q, k] = total.astype(bf)
            return carry

        lax.fori_loop(0, n_z, core_sum, 0)
        stage_d.append([
            remote(sum_c.at[f, p[0]], got_d.at[f, i], ds.at[f, i], dr.at[f, i], p)
            for i, p in enumerate(along_dp)
        ])
        for copy in stage_d[f]:
            copy.start()
    stage_z = []
    for f in range(count):
        for copy in stage_d[f]:
            copy.wait()

        def dp_sum(k, carry):
            total = sum_c[f, d, k].astype(f32)
            for i in range(n_dp - 1):
                total += got_d[f, i, k].astype(f32)
            sum_d[f, k] = total.astype(bf)
            return carry

        lax.fori_loop(0, n_z, dp_sum, 0)
        stage_z.append([
            remote(sum_d.at[f, lax.rem(z + i + 1, n_z)], got_z.at[f, i], zs.at[f, i], zr.at[f, i], p)
            for i, p in enumerate(along_z)
        ])
        for copy in stage_z[f]:
            copy.start()
    for f in range(count):
        for copy in stage_z[f]:
            copy.wait()
        total = sum_d[f, z].astype(f32)
        for i in range(n_z - 1):
            total += got_z[f, i].astype(f32)
        outs[f][...] = total


def reduce_all(grads, n_dp, n_z):
    count = len(grads)
    blocks, rows, cols = grads[0].shape
    own, strip = blocks // (2 * n_z), rows // n_dp
    bf = jnp.bfloat16
    parts = [g.astype(bf).reshape(n_z, 2, own, n_dp, strip, cols) for g in grads]
    dma = pltpu.SemaphoreType.DMA
    piece = (own, strip, cols)
    return pl.pallas_call(
        lambda *refs: reduce_kernel(n_dp, n_z, count, *refs),
        out_shape=[jax.ShapeDtypeStruct(piece, jnp.float32)] * count,
        in_specs=[pl.BlockSpec(memory_space=pl.ANY)] * count,
        out_specs=[pl.BlockSpec(memory_space=pltpu.VMEM)] * count,
        scratch_shapes=[
            pltpu.VMEM((count, n_z, own, n_dp, strip, cols), bf),
            pltpu.VMEM((count, n_z, own, n_dp, strip, cols), bf),
            pltpu.VMEM((count, n_dp, n_z) + piece, bf),
            pltpu.VMEM((count, n_dp - 1, n_z) + piece, bf),
            pltpu.VMEM((count, n_z) + piece, bf),
            pltpu.VMEM((count, n_z - 1) + piece, bf),
            dma((count,)),
            dma((count,)),
            dma((count,)),
            dma((count, n_dp - 1)),
            dma((count, n_dp - 1)),
            dma((count, n_z - 1)),
            dma((count, n_z - 1)),
        ],
        compiler_params=pltpu.CompilerParams(
            collective_id=1, has_side_effects=True, vmem_limit_bytes=40 * 2**20
        ),
        cost_estimate=pl.CostEstimate(flops=0, bytes_accessed=64 * 2**20, transcendentals=0),
    )(*parts)


def to_tokens(values):
    return lax.all_to_all(values, "tensor", split_axis=0, concat_axis=1, tiled=True)


def to_blocks(values):
    return lax.all_to_all(values, "tensor", split_axis=1, concat_axis=0, tiled=True)


def make(n_dp, n_z):
    def on_device(tokens_in, right_one, left_one, right_two, left_two, out_grad):
        bf = jnp.bfloat16
        f32 = jnp.float32

        def dot(spec, a, b):
            return jnp.einsum(spec, a, b, preferred_element_type=f32)

        u1 = dot("tbi,bio->tbo", tokens_in, right_one).astype(bf)
        (left_one, right_two, left_two), v1 = gather_and_swap(
            u1, (left_one, right_two, left_two), n_dp, n_z
        )
        v1 = jnp.swapaxes(v1, 0, 1).reshape(v1.shape[1], -1, v1.shape[3])
        v1, late_grad = lax.optimization_barrier((v1, out_grad))
        dw_two = to_tokens(late_grad)
        z1 = dot("tbj,jbk->tjk", v1, left_one).astype(bf)
        hidden = gelu_value(z1.astype(f32)).astype(bf)
        u2 = dot("tjk,kjm->tkm", hidden, right_two).astype(bf)
        w2 = dot("tkm,mkn->tnm", u2, left_two).astype(bf)
        mixed = to_blocks(w2)
        layer_out = (tokens_in.astype(f32) + mixed.astype(f32)).astype(bf)
        du2 = dot("tnm,mkn->tkm", dw_two, left_two).astype(bf)
        gl2 = dot("tkm,tnm->mkn", u2, dw_two)
        gr2 = dot("tjk,tkm->kjm", hidden, du2)
        dh = dot("tkm,kjm->tjk", du2, right_two)
        dz1 = (dh * gelu_slope(z1.astype(f32))).astype(bf)
        dv1 = dot("tjk,jbk->tbj", dz1, left_one).astype(bf)
        du1 = to_blocks(dv1)
        gl1 = dot("tbj,tjk->jbk", v1, dz1)
        gl2, gr2, gl1 = reduce_all((gl2, gr2, gl1), n_dp, n_z)
        gr1 = dot("tbi,tbo->bio", tokens_in, du1)
        input_grad = (out_grad.astype(f32) + dot("tbo,bio->tbi", du1, right_one)).astype(bf)
        gr1 = gr1.astype(bf).reshape(gr1.shape[0], n_dp, -1, gr1.shape[2])
        gr1 = lax.all_to_all(gr1, "dp", split_axis=1, concat_axis=1, tiled=True)
        gr1 = jnp.sum(gr1.astype(f32), axis=1)
        return (layer_out, input_grad, gr1, gl1, gr2, gl2)

    return on_device


def solution(mesh):
    split = P("dp", "tensor", None)
    factor = P("tensor", None, None)
    grad = P("tensor", "dp", None)
    return jax.shard_map(
        make(mesh.shape["dp"], mesh.shape["tensor"] // 2),
        mesh=mesh,
        in_specs=(split, factor, factor, factor, factor, split),
        out_specs=(split, split, grad, grad, grad, grad),
        check_vma=False,
    )
```

time: 572 us -> 392 us (0.69); the launches traced: 565 us -> 391 us
  waiting for transfers between devices: 344 us -> 62.6 us
  Pallas kernels: 0 us -> 187 us
  blocking collectives: 50.1 us -> 0 us
  matrix products: 60.9 us -> 46.8 us
  between operations: 14.3 us -> 0.81 us
    pallas_call x0 -> x2, Pallas kernels: none -> 187 us  [the longest x1 96.5 us: gather_and_swap(): pl.pallas_call(lambda *refs: gather_kernel(n_dp, n_z, count, *refs), out_...]
    reduce_scatter x7 -> x0, waiting for transfers between devices: 174 us -> none  [the longest x3 91.5 us: reduce_all(): lax.psum_scatter(grad, 'tensor', scatter_dimension=0, tiled=True)]
    all_gather x3 -> x0, waiting for transfers between devices: 77.6 us -> none  [gather_factor(): whole = lax.all_gather(mine, ('tensor', 'dp'), axis=0, tiled=True)]
    all_to_all x2 -> x1, waiting for transfers between devices: 91.6 us -> 40.4 us  [to_tokens(): lax.all_to_all(values, 'tensor', split_axis=0, concat_axis=1, tiled=True)]
    all_to_all x1 -> x0, blocking collectives: 50.1 us -> none  [to_blocks(): lax.all_to_all(values, 'tensor', split_axis=1, concat_axis=0, tiled=True)]
    all_to_all x1 -> x2, waiting for transfers between devices: 0.01 us -> 21.1 us  [to_blocks(): lax.all_to_all(values, 'tensor', split_axis=1, concat_axis=0, tiled=True)]
    dot_general x12, matrix products: 60.9 us -> 46.8 us  [dot(): return jnp.einsum(spec, a, b, preferred_element_type=f32)]
    all_to_all x2 -> x1, starting transfers between devices: 13.4 us -> 4.31 us  [to_tokens(): lax.all_to_all(values, 'tensor', split_axis=0, concat_axis=1, tiled=True)]
  transfers between devices with their start and end apart: 13 -> 4, of which waited for: 10 -> 3; matrix products, arithmetic and copies ran while one was open for 17% -> 12% of each run, Pallas kernels for 0% -> 23%
where the time goes in v1:
time: 392 us; the launch traced here: 391 us
  Pallas kernels  187 us (48%)
  local copies, waits for them, and re-layouts  65.8 us (17%)
  waiting for transfers between devices  62.6 us (16%)
  matrix products  46.8 us (12%)
  starting transfers between devices  24.1 us (6%)
  other arithmetic  4.17 us (1%)
    pallas_call x1, Pallas kernels, gather_and_swap(): pl.pallas_call(lambda *refs: gather_kernel(n_dp, n_z, count, *refs), out_...  96.5 us
    pallas_call x1, Pallas kernels, reduce_all(): pl.pallas_call(lambda *refs: reduce_kernel(n_dp, n_z, count, *refs), out_...  90.6 us
    dot_general x12, matrix products, dot(): return jnp.einsum(spec, a, b, preferred_element_type=f32)  46.8 us
    all_to_all x1, waiting for transfers between devices, to_tokens(): lax.all_to_all(values, 'tensor', split_axis=0, concat_axis=1, tiled=True)  40.4 us
    all_to_all x2, waiting for transfers between devices, to_blocks(): lax.all_to_all(values, 'tensor', split_axis=1, concat_axis=0, tiled=True)  21.1 us
    all_to_all x2, starting transfers between devices, to_blocks(): lax.all_to_all(values, 'tensor', split_axis=1, concat_axis=0, tiled=True)  15.7 us
    unnamed x23, local copies, waits for them, and re-layouts  11.6 us
  transfers between devices with their start and end apart: 4, of which 3 were waited for; matrix products, arithmetic and copies ran while one was open for 12% of the time, Pallas kernels for 23%

profile of v1, /device:TPU:8, one launch (start us, length us, event | category | flops | bytes accessed | tf_op | source)
XLA Modules:
  0.0 391.3 jit_solution(10755911256784200737)
XLA Ops:
  5.8 4.5 %copy.100 = bf16[512,16,128]{2,1,0:T(8,128)(2,1)} copy(bf16[512,16,128]{0,2,1:T(8,128)(2,1)} %convert_bitcast_fusion.4) | data formatting | bytes 4194304 | tf_op jit(solution)/shard_map/convert_element_type | solution.py:240
  10.3 96.5 %shard_map.109 = (bf16[4,2,4,512,128]{4,3,2,1,0:T(8,128)(2,1)}, bf16[4,2,4,512,128]{4,3,2,1,0:T(8,128)(2,1)}, bf16[4,2,4,512,128]{4,3,2,1,0:T(8,128)(2,1)}, bf16[8,64,16,128]{3,2,1,0:T(8,128)(2,1)}) custom-call(bf16[4,512,128]{2,1,0:T(8,128)(2,1)} %bitcast.102, bf16[4,512,128]{2,1,0:T(8,128)(2,1)} %bitcast.103, bf16[4,512,128]{2,1,0:T(8,128)(2,1)} %bitcast.104, ...), custom_call_target="tpu_custom_call" | custom-call | bytes 67108864 | tf_op jit(solution)/shard_map/pallas_call | solution.py:106
  110.3 4.3 %all-to-all-start.1 = ((bf16[512,16,128]{2,1,0:T(8,128)(2,1)}), bf16[512,16,128]{2,1,0:T(8,128)(2,1)}, u32[]{:S(2)}, u32[]{:S(2)}) async-start(bf16[512,16,128]{2,1,0:T(8,128)(2,1)} %param.11), calls=%async_computation.1 | async-start | bytes 4194304 | tf_op jit(solution)/shard_map/all_to_all | solution.py:225
  114.6 4.2 %copy.102 = bf16[64,128,128]{1,0,2:T(8,128)(2,1)} copy(bf16[64,128,128]{2,1,0:T(8,128)(2,1)} %bitcast.96) | data formatting | bytes 4194304 | tf_op jit(solution)/shard_map/optimization_barrier | solution.py:245
  118.8 40.4 %all-to-all-done.1 = bf16[512,16,128]{2,1,0:T(8,128)(2,1)} async-done(((bf16[512,16,128]{2,1,0:T(8,128)(2,1)}), bf16[512,16,128]{2,1,0:T(8,128)(2,1)}, u32[]{:S(2)}, u32[]{:S(2)}) %all-to-all-start.1) | async-done | bytes 2097184 | tf_op jit(solution)/shard_map/all_to_all | solution.py:225
  162.8 4.1 %copy.110 = bf16[64,128,128]{1,0,2:T(8,128)(2,1)} copy(bf16[64,128,128]{2,1,0:T(8,128)(2,1)} %bitcast.97) | data formatting | bytes 4194304 | tf_op jit(solution)/shard_map/all_to_all | solution.py:225
  166.9 7.2 %convolution_convert_fusion.4 = bf16[128,128,64]{1,2,0:T(8,128)(2,1)} fusion(bf16[128,128,128]{2,1,0:T(8,128)(2,1)} %bitcast.90, bf16[64,128,128]{1,0,2:T(8,128)(2,1)} %copy.110), kind=kOutput, calls=%fused_computation.26 | convolution fusion | flops 269484032 | bytes 8388608 | tf_op jit(solution)/shard_map/tnm,mkn->tkm/dot_general | solution.py:238
  174.0 4.6 %copy.111 = bf16[128,128,64]{0,2,1:T(8,128)(2,1)} copy(bf16[128,128,64]{1,2,0:T(8,128)(2,1)} %convolution_convert_fusion.4) | data formatting | bytes 4194304 | tf_op jit(solution)/shard_map/convert_element_type | solution.py:253
  178.6 7.8 %fusion.12 = f32[128,128,64]{1,2,0:T(8,128)} fusion(bf16[128,128,128]{2,1,0:T(8,128)(2,1)} %bitcast.92, bf16[128,128,64]{0,2,1:T(8,128)(2,1)} %copy.111), kind=kOutput, calls=%fused_computation.29 | convolution fusion | flops 268435456 | bytes 10485760 | tf_op jit(solution)/shard_map/tkm,kjm->tjk/dot_general | solution.py:238
  186.4 5.5 %copy.112 = f32[128,128,64]{0,2,1:T(8,128)} copy(f32[128,128,64]{1,2,0:T(8,128)} %fusion.12) | data formatting | bytes 8388608 | tf_op jit(solution)/shard_map/tkm,kjm->tjk/dot_general | solution.py:238
  191.8 6.8 %fusion.5 = (bf16[64,128,128]{2,0,1:T(8,128)(2,1)S(1)}, bf16[64,128,128]{2,0,1:T(8,128)(2,1)}) fusion(f32[128,128,64]{0,2,1:T(8,128)} %copy.112, bf16[64,128,128]{1,0,2:T(8,128)(2,1)} %copy.102, bf16[128,128,128]{2,1,0:T(8,128)(2,1)} %bitcast.98), kind=kOutput, calls=%fused_computation.6 | convolution fusion | flops 284164096 | bytes 14680064 | tf_op jit(solution)/shard_map/tbj,jbk->tjk/dot_general | solution.py:238
  200.0 4.4 %convert_bitcast_fusion.1 = bf16[64,128,128]{1,0,2:T(8,128)(2,1)} fusion(bf16[128,128,128]{2,1,0:T(8,128)(2,1)S(1)} %bitcast.99, bf16[64,128,128]{2,0,1:T(8,128)(2,1)S(1)} %get-tuple-element.54), kind=kOutput, calls=%fused_computation.21 | convolution fusion | flops 269484032 | bytes 8388608 | tf_op jit(solution)/shard_map/tjk,jbk->tbj/dot_general | solution.py:238
  204.3 4.5 %copy.113 = bf16[64,128,128]{2,0,1:T(8,128)(2,1)} copy(bf16[64,128,128]{1,0,2:T(8,128)(2,1)} %convert_bitcast_fusion.1) | data formatting | bytes 4194304 | tf_op jit(solution)/shard_map/convert_element_type | solution.py:258
  208.8 7.8 %all-to-all-start.2 = ((bf16[64,128,128]{2,0,1:T(8,128)(2,1)}), bf16[64,128,128]{2,0,1:T(8,128)(2,1)}, u32[]{:S(2)}, u32[]{:S(2)}) async-start(bf16[64,128,128]{2,0,1:T(8,128)(2,1)} %copy.113), calls=%async_computation.2 | async-start | bytes 4194304 | tf_op jit(solution)/shard_map/all_to_all | solution.py:229
  216.7 4.6 %copy.103 = bf16[64,128,128]{1,0,2:T(8,128)(2,1)} copy(bf16[64,128,128]{2,0,1:T(8,128)(2,1)} %get-tuple-element.55) | data formatting | bytes 4194304 | tf_op jit(solution)/shard_map/convert_element_type | solution.py:248
  221.3 5.4 %convert_bitcast_fusion.3 = bf16[64,128,128]{2,0,1:T(8,128)(2,1)} fusion(bf16[64,128,128]{1,0,2:T(8,128)(2,1)} %copy.103, bf16[128,128,128]{2,1,0:T(8,128)(2,1)} %bitcast.93), kind=kOutput, calls=%fused_computation.23 | convolution fusion | flops 269484032 | bytes 8388608 | tf_op jit(solution)/shard_map/tjk,kjm->tkm/dot_general | solution.py:238
  226.6 4.6 %copy.104 = bf16[64,128,128]{1,0,2:T(8,128)(2,1)} copy(bf16[64,128,128]{2,0,1:T(8,128)(2,1)} %convert_bitcast_fusion.3) | data formatting | bytes 4194304 | tf_op jit(solution)/shard_map/convert_element_type | solution.py:249
  231.2 5.4 %convert_bitcast_fusion.2 = bf16[64,128,128]{1,0,2:T(8,128)(2,1)} fusion(bf16[64,128,128]{1,0,2:T(8,128)(2,1)} %copy.104, bf16[128,128,128]{2,1,0:T(8,128)(2,1)} %bitcast.91), kind=kOutput, calls=%fused_computation.22 | convolution fusion | flops 269484032 | bytes 8388608 | tf_op jit(solution)/shard_map/tkm,mkn->tnm/dot_general | solution.py:238
  236.6 4.6 %copy.105 = bf16[64,128,128]{2,0,1:T(8,128)(2,1)} copy(bf16[64,128,128]{1,0,2:T(8,128)(2,1)} %convert_bitcast_fusion.2) | data formatting | bytes 4194304 | tf_op jit(solution)/shard_map/convert_element_type | solution.py:250
  241.1 21.1 %all-to-all-done.2 = bf16[64,128,128]{2,0,1:T(8,128)(2,1)} async-done(((bf16[64,128,128]{2,0,1:T(8,128)(2,1)}), bf16[64,128,128]{2,0,1:T(8,128)(2,1)}, u32[]{:S(2)}, u32[]{:S(2)}) %all-to-all-start.2) | async-done | bytes 2097184 | tf_op jit(solution)/shard_map/all_to_all | solution.py:229
  262.2 7.8 %all-to-all-start = ((bf16[64,128,128]{2,0,1:T(8,128)(2,1)}), bf16[64,128,128]{2,0,1:T(8,128)(2,1)}, u32[]{:S(2)}, u32[]{:S(2)}) async-start(bf16[64,128,128]{2,0,1:T(8,128)(2,1)} %copy.105), calls=%async_computation | async-start | bytes 4194304 | tf_op jit(solution)/shard_map/all_to_all | solution.py:229
  270.1 3.7 convolution_convert_fusion.2
  277.4 90.6 %shard_map.110 = (f32[16,32,128]{2,1,0:T(8,128)S(1)}, f32[16,32,128]{2,1,0:T(8,128)S(1)}, f32[16,32,128]{2,1,0:T(8,128)S(1)}) custom-call(bf16[4,2,16,4,32,128]{5,4,3,2,1,0:T(8,128)(2,1)S(1)} %bitcast.85, bf16[4,2,16,4,32,128]{5,4,3,2,1,0:T(8,128)(2,1)S(1)} %bitcast.86, bf16[4,2,16,4,32,128]{5,4,3,2,1,0:T(8,128)(2,1)S(1)} %bitcast.87), custom_call_target="tpu_custom_call" | custom-call | bytes 67108864 | tf_op jit(solution)/shard_map/pallas_call | solution.py:197
  375.3 4.1 %all-to-all-start.3 = ((bf16[16,4,32,128]{3,2,0,1:T(8,128)(2,1)}), bf16[16,4,32,128]{3,2,0,1:T(8,128)(2,1)}, u32[]{:S(2)}, u32[]{:S(2)}) async-start(bf16[16,4,32,128]{3,2,0,1:T(8,128)(2,1)} %copy.117), calls=%async_computation.3 | async-start | bytes 1048576 | tf_op jit(solution)/shard_map/all_to_all | solution.py:265
  (39 shorter events, 36.2 us)
Async XLA Ops:
  0.6 3.1 copy-start
  110.3 48.9 %all-to-all-start.1 = ((bf16[512,16,128]{2,1,0:T(8,128)(2,1)}), bf16[512,16,128]{2,1,0:T(8,128)(2,1)}, u32[]{:S(2)}, u32[]{:S(2)}) async-start(bf16[512,16,128]{2,1,0:T(8,128)(2,1)} %param.11), calls=%async_computation.1 | async-start | bytes 4194304 | tf_op jit(solution)/shard_map/all_to_all | solution.py:225
  191.8 8.1 %copy-start.8 = (bf16[4,2,4,512,128]{4,3,2,1,0:T(8,128)(2,1)S(1)}, bf16[4,2,4,512,128]{4,3,2,1,0:T(8,128)(2,1)}, u32[]{:S(2)}) copy-start(bf16[4,2,4,512,128]{4,3,2,1,0:T(8,128)(2,1)} %get-tuple-element.17) | copy-start | bytes 12582916
  198.6 1.3 copy-start.6
  208.8 53.4 %all-to-all-start.2 = ((bf16[64,128,128]{2,0,1:T(8,128)(2,1)}), bf16[64,128,128]{2,0,1:T(8,128)(2,1)}, u32[]{:S(2)}, u32[]{:S(2)}) async-start(bf16[64,128,128]{2,0,1:T(8,128)(2,1)} %copy.113), calls=%async_computation.2 | async-start | bytes 4194304 | tf_op jit(solution)/shard_map/all_to_all | solution.py:229
  262.2 113.1 %all-to-all-start = ((bf16[64,128,128]{2,0,1:T(8,128)(2,1)}), bf16[64,128,128]{2,0,1:T(8,128)(2,1)}, u32[]{:S(2)}, u32[]{:S(2)}) async-start(bf16[64,128,128]{2,0,1:T(8,128)(2,1)} %copy.105), calls=%async_computation | async-start | bytes 4194304 | tf_op jit(solution)/shard_map/all_to_all | solution.py:229
  270.1 3.7 copy-start.1
  270.1 3.7 copy-start.2
  273.8 1.6 copy-start.5
  273.8 2.2 copy-start.7
  368.0 2.2 copy-start.3
  375.3 12.1 %all-to-all-start.3 = ((bf16[16,4,32,128]{3,2,0,1:T(8,128)(2,1)}), bf16[16,4,32,128]{3,2,0,1:T(8,128)(2,1)}, u32[]{:S(2)}, u32[]{:S(2)}) async-start(bf16[16,4,32,128]{3,2,0,1:T(8,128)(2,1)} %copy.117), calls=%async_computation.3 | async-start | bytes 1048576 | tf_op jit(solution)/shard_map/all_to_all | solution.py:265
  383.0 1.6 copy-start.4

commit v2 on v1

--- a/solution.py
+++ b/solution.py
@@ -46,44 +46,65 @@
     )
 
 
+def halves_of(n_dp):
+    return 2, n_dp // 2
+
+
 def gather_kernel(n_dp, n_z, count, *refs):
     shards, (sent, wholes), sems = refs[:count], (refs[count], refs[count + 1 : 2 * count + 1]), refs[2 * count + 1 :]
     got = sems[0]
-    own_sem, zs, zr, ds, dr, cs, cr, us, ur, ul = sems[1:]
+    own_sem, zs, zr, ls, lr, hs, hr, cs, cr, us, ur, ul = sems[1:]
+    n_hi, n_lo = halves_of(n_dp)
     d, z, c = place()
     n = n_z * 2
     rank = z * 2 + c
     along_z, along_dp, sibling = peers_of(n_dp, n_z)
     others = [lax.rem(rank + k, n) for k in range(1, n)]
-    greet([(d, p) for p in others] + along_dp)
+    hi, lo = lax.div(d, n_lo), lax.rem(d, n_lo)
+    along_lo = [(hi * n_lo + lax.rem(lo + k, n_lo), rank) for k in range(1, n_lo)]
+    along_hi = [(lax.rem(hi + k, n_hi) * n_lo + lo, rank) for k in range(1, n_hi)]
+    greet([(d, p) for p in others] + along_lo + along_hi)
     swaps = [remote(sent.at[p], got.at[rank], us.at[i], ur.at[i], (d, p)) for i, p in enumerate(others)]
     keep = pltpu.make_async_copy(sent.at[rank], got.at[rank], ul)
     stage_z, own = [], []
     for f in range(count):
-        own.append(pltpu.make_async_copy(shards[f].at[d], wholes[f].at[z, c, d], own_sem.at[f]))
+        own.append(pltpu.make_async_copy(shards[f].at[d], wholes[f].at[z, c, hi, lo], own_sem.at[f]))
         stage_z.append([
-            remote(shards[f].at[d], wholes[f].at[z, c, d], zs.at[f, i], zr.at[f, i], p)
+            remote(shards[f].at[d], wholes[f].at[z, c, hi, lo], zs.at[f, i], zr.at[f, i], p)
             for i, p in enumerate(along_z)
         ])
     for f in range(count):
         own[f].start()
         for copy in stage_z[f]:
             copy.start()
-    stage_dp = []
+
+    def spread(f, stage, lo_part, hi_part):
+        copies = [
+            remote(lo_part, lo_part, ls.at[f, stage, i], lr.at[f, stage, i], p) for i, p in enumerate(along_lo)
+        ] + [
+            remote(hi_part, hi_part, hs.at[f, stage, i], hr.at[f, stage, i], p) for i, p in enumerate(along_hi)
+        ]
+        for copy in copies:
+            copy.start()
+        return copies
+
+    first = []
     for f in range(count):
         own[f].wait()
         for copy in stage_z[f]:
             copy.wait()
-        part = wholes[f].at[:, c, d]
-        stage_dp.append([remote(part, part, ds.at[f, i], dr.at[f, i], p) for i, p in enumerate(along_dp)])
-        for copy in stage_dp[f]:
-            copy.start()
+        first.append(spread(f, 0, wholes[f].at[:, c, hi, lo, 0], wholes[f].at[:, c, hi, lo, 1]))
     keep.start()
     for copy in swaps:
         copy.start()
+    second = []
+    for f in range(count):
+        for copy in first[f]:
+            copy.wait()
+        second.append(spread(f, 1, wholes[f].at[:, c, :, lo, 1], wholes[f].at[:, c, hi, :, 0]))
     stage_core = []
     for f in range(count):
-        for copy in stage_dp[f]:
+        for copy in second[f]:
             copy.wait()
         half = wholes[f].at[:, c]
         stage_core.append(remote(half, half, cs.at[f], cr.at[f], sibling))
@@ -99,13 +120,14 @@
     count, n = len(factors), n_z * 2
     blocks, rows, cols = factors[0].shape
     part = blocks * rows // n_dp
-    shards = [f.reshape(n_dp, part, cols) for f in factors]
+    n_hi, n_lo = halves_of(n_dp)
+    shards = [f.reshape(n_dp, 2, part // 2, cols) for f in factors]
     sent = values.reshape((n, values.shape[0] // n) + values.shape[1:])
     dma = pltpu.SemaphoreType.DMA
     hbm = pl.BlockSpec(memory_space=pl.ANY)
     out = pl.pallas_call(
         lambda *refs: gather_kernel(n_dp, n_z, count, *refs),
-        out_shape=[jax.ShapeDtypeStruct((n_z, 2, n_dp, part, cols), f.dtype) for f in factors]
+        out_shape=[jax.ShapeDtypeStruct((n_z, 2, n_hi, n_lo, 2, part // 2, cols), f.dtype) for f in factors]
         + [jax.ShapeDtypeStruct(sent.shape, sent.dtype)],
         in_specs=[hbm] * (count + 1),
         out_specs=[hbm] * (count + 1),
@@ -113,8 +135,10 @@
             dma((count,)),
             dma((count, n_z - 1)),
             dma((count, n_z - 1)),
-            dma((count, n_dp - 1)),
-            dma((count, n_dp - 1)),
+            dma((count, 2, n_lo - 1)),
+            dma((count, 2, n_lo - 1)),
+            dma((count, 2, n_hi - 1)),
+            dma((count, 2, n_hi - 1)),
             dma((count,)),
             dma((count,)),
             dma((n - 1,)),
@@ -248,6 +272,7 @@
         hidden = gelu_value(z1.astype(f32)).astype(bf)
         u2 = dot("tjk,kjm->tkm", hidden, right_two).astype(bf)
         w2 = dot("tkm,mkn->tnm", u2, left_two).astype(bf)
+        dw_two, w2 = lax.optimization_barrier((dw_two, w2))
         mixed = to_blocks(w2)
         layer_out = (tokens_in.astype(f32) + mixed.astype(f32)).astype(bf)
         du2 = dot("tnm,mkn->tkm", dw_two, left_two).astype(bf)
@@ -256,8 +281,9 @@
         dh = dot("tkm,kjm->tjk", du2, right_two)
         dz1 = (dh * gelu_slope(z1.astype(f32))).astype(bf)
         dv1 = dot("tjk,jbk->tbj", dz1, left_one).astype(bf)
+        gl1 = dot("tbj,tjk->jbk", v1, dz1)
+        dv1, gl2, gr2, gl1 = lax.optimization_barrier((dv1, gl2.astype(bf), gr2.astype(bf), gl1.astype(bf)))
         du1 = to_blocks(dv1)
-        gl1 = dot("tbj,tjk->jbk", v1, dz1)
         gl2, gr2, gl1 = reduce_all((gl2, gr2, gl1), n_dp, n_z)
         gr1 = dot("tbi,tbo->bio", tokens_in, du1)
         input_grad = (out_grad.astype(f32) + dot("tbo,bio->tbi", du1, right_one)).astype(bf)

time: 392 us -> 388 us (0.990)
  Pallas kernels: 187 us -> 175 us
  waiting for transfers between devices: 62.6 us -> 57.5 us
  local copies, waits for them, and re-layouts: 65.8 us -> 70.2 us
  other arithmetic: 4.17 us -> 8.34 us
    all_to_all x1, waiting for transfers between devices: 40.4 us -> 15.5 us  [to_tokens(): lax.all_to_all(values, 'tensor', split_axis=0, concat_axis=1, tiled=True)]
    all_to_all x2, waiting for transfers between devices: 21.1 us -> 41.1 us  [to_blocks(): lax.all_to_all(values, 'tensor', split_axis=1, concat_axis=0, tiled=True)]
    optimization_barrier x0 -> x3, local copies, waits for them, and re-layouts: none -> 13.3 us  [the longest x2 8.69 us: on_device(): dw_two, w2 = lax.optimization_barrier((dw_two, w2))]
    pallas_call x1, Pallas kernels: 96.5 us -> 84.8 us  [gather_and_swap(): pl.pallas_call(lambda *refs: gather_kernel(n_dp, n_z, count, *refs), out_...]
    convert_element_type x2 -> x0, local copies, waits for them, and re-layouts: 9.1 us -> none  [the longest x1 4.56 us: on_device(): w2 = dot('tkm,mkn->tnm', u2, left_two).astype(bf)]
    unnamed x23 -> x29, local copies, waits for them, and re-layouts: 11.6 us -> 15.9 us
    convert_element_type x0 -> x1, other arithmetic: none -> 4.17 us  [on_device(): dz1 = (dh * gelu_slope(z1.astype(f32))).astype(bf)]
    all_to_all x2 -> x1, local copies, waits for them, and re-layouts: 7.62 us -> 3.55 us  [to_tokens(): lax.all_to_all(values, 'tensor', split_axis=0, concat_axis=1, tiled=True)]
where the time goes in v2:
time: 388 us; the launch traced here: 387 us
  Pallas kernels  175 us (45%)
  local copies, waits for them, and re-layouts  70.2 us (18%)
  waiting for transfers between devices  57.5 us (15%)
  matrix products  49.8 us (13%)
  starting transfers between devices  25.1 us (6%)
  other arithmetic  8.34 us (2%)
    pallas_call x1, Pallas kernels, reduce_all(): pl.pallas_call(lambda *refs: reduce_kernel(n_dp, n_z, count, *refs), out_...  90.3 us
    pallas_call x1, Pallas kernels, gather_and_swap(): pl.pallas_call(lambda *refs: gather_kernel(n_dp, n_z, count, *refs), out_...  84.8 us
    dot_general x12, matrix products, dot(): return jnp.einsum(spec, a, b, preferred_element_type=f32)  49.8 us
    all_to_all x2, waiting for transfers between devices, to_blocks(): lax.all_to_all(values, 'tensor', split_axis=1, concat_axis=0, tiled=True)  41.1 us
    unnamed x29, local copies, waits for them, and re-layouts  15.9 us
    all_to_all x2, starting transfers between devices, to_blocks(): lax.all_to_all(values, 'tensor', split_axis=1, concat_axis=0, tiled=True)  15.7 us
    all_to_all x1, waiting for transfers between devices, to_tokens(): lax.all_to_all(values, 'tensor', split_axis=0, concat_axis=1, tiled=True)  15.5 us
    optimization_barrier x2, local copies, waits for them, and re-layouts, on_device(): dw_two, w2 = lax.optimization_barrier((dw_two, w2))  8.69 us
  transfers between devices with their start and end apart: 4, of which 3 were waited for; matrix products, arithmetic and copies ran while one was open for 12% of the time, Pallas kernels for 23%

profile of v2, /device:TPU:8, one launch (start us, length us, event | category | flops | bytes accessed | tf_op | source)
XLA Modules:
  0.0 386.8 jit_solution(14257881114521395758)
XLA Ops:
  5.8 4.5 %copy.100 = bf16[512,16,128]{2,1,0:T(8,128)(2,1)} copy(bf16[512,16,128]{0,2,1:T(8,128)(2,1)} %convert_bitcast_fusion.4) | data formatting | bytes 4194304 | tf_op jit(solution)/shard_map/convert_element_type | solution.py:264
  10.3 84.8 %shard_map.109 = (bf16[4,2,2,2,2,256,128]{6,5,4,3,2,1,0:T(8,128)(2,1)}, bf16[4,2,2,2,2,256,128]{6,5,4,3,2,1,0:T(8,128)(2,1)}, bf16[4,2,2,2,2,256,128]{6,5,4,3,2,1,0:T(8,128)(2,1)}, bf16[8,64,16,128]{3,2,1,0:T(8,128)(2,1)}) custom-call(bf16[4,2,256,128]{3,2,1,0:T(8,128)(2,1)} %bitcast.102, bf16[4,2,256,128]{3,2,1,0:T(8,128)(2,1)} %bitcast.103, ...), custom_call_target="tpu_custom_call" | custom-call | bytes 67108864 | tf_op jit(solution)/shard_map/pallas_call | solution.py:128
  98.6 5.0 %all-to-all-start = ((bf16[512,16,128]{2,1,0:T(8,128)(2,1)}), bf16[512,16,128]{2,1,0:T(8,128)(2,1)}, u32[]{:S(2)}, u32[]{:S(2)}) async-start(bf16[512,16,128]{2,1,0:T(8,128)(2,1)} %param.11), calls=%async_computation | async-start | bytes 4194304 | tf_op jit(solution)/shard_map/all_to_all | solution.py:249
  103.7 4.1 %copy.103 = bf16[64,128,128]{1,0,2:T(8,128)(2,1)} copy(bf16[64,128,128]{2,1,0:T(8,128)(2,1)} %bitcast.98) | data formatting | bytes 4194304 | tf_op jit(solution)/shard_map/optimization_barrier | solution.py:269
  107.8 6.1 %fusion.9 = (bf16[64,128,128]{2,0,1:T(8,128)(2,1)}, bf16[128,128,64]{1,2,0:T(8,128)(2,1)}) fusion(bf16[64,128,128]{1,0,2:T(8,128)(2,1)} %copy.103, bf16[128,128,128]{2,1,0:T(8,128)(2,1)} %bitcast.90), kind=kOutput, calls=%fused_computation.15 | convolution fusion | flops 275775488 | bytes 10485760 | tf_op jit(solution)/shard_map/tbj,jbk->tjk/dot_general | solution.py:262
  113.8 4.6 %copy.104 = bf16[64,128,128]{1,0,2:T(8,128)(2,1)} copy(bf16[64,128,128]{2,0,1:T(8,128)(2,1)} %get-tuple-element.66) | data formatting | bytes 4194304 | tf_op jit(solution)/shard_map/convert_element_type | solution.py:272
  118.4 5.4 %convert_bitcast_fusion.3 = bf16[64,128,128]{2,0,1:T(8,128)(2,1)} fusion(bf16[64,128,128]{1,0,2:T(8,128)(2,1)} %copy.104, bf16[128,128,128]{2,1,0:T(8,128)(2,1)} %bitcast.92), kind=kOutput, calls=%fused_computation.23 | convolution fusion | flops 269484032 | bytes 8388608 | tf_op jit(solution)/shard_map/tjk,kjm->tkm/dot_general | solution.py:262
  123.8 4.6 %copy.105 = bf16[64,128,128]{1,0,2:T(8,128)(2,1)} copy(bf16[64,128,128]{2,0,1:T(8,128)(2,1)} %convert_bitcast_fusion.3) | data formatting | bytes 4194304 | tf_op jit(solution)/shard_map/convert_element_type | solution.py:273
  128.4 5.4 %convert_bitcast_fusion.2 = bf16[64,128,128]{1,0,2:T(8,128)(2,1)} fusion(bf16[64,128,128]{1,0,2:T(8,128)(2,1)} %copy.105, bf16[128,128,128]{2,1,0:T(8,128)(2,1)} %bitcast.94), kind=kOutput, calls=%fused_computation.22 | convolution fusion | flops 269484032 | bytes 8388608 | tf_op jit(solution)/shard_map/tkm,mkn->tnm/dot_general | solution.py:262
  133.7 15.5 %all-to-all-done = bf16[512,16,128]{2,1,0:T(8,128)(2,1)} async-done(((bf16[512,16,128]{2,1,0:T(8,128)(2,1)}), bf16[512,16,128]{2,1,0:T(8,128)(2,1)}, u32[]{:S(2)}, u32[]{:S(2)}) %all-to-all-start) | async-done | bytes 2097184 | tf_op jit(solution)/shard_map/all_to_all | solution.py:249
  152.8 4.2 %copy.110 = bf16[64,128,128]{1,0,2:T(8,128)(2,1)} copy(bf16[64,128,128]{2,1,0:T(8,128)(2,1)} %bitcast.99) | data formatting | bytes 4194304 | tf_op jit(solution)/shard_map/optimization_barrier | solution.py:275
  157.0 7.2 %convolution_convert_fusion.4 = bf16[128,128,64]{1,2,0:T(8,128)(2,1)} fusion(bf16[128,128,128]{2,1,0:T(8,128)(2,1)} %bitcast.95, bf16[64,128,128]{1,0,2:T(8,128)(2,1)} %copy.110), kind=kOutput, calls=%fused_computation.26 | convolution fusion | flops 269484032 | bytes 8388608 | tf_op jit(solution)/shard_map/tnm,mkn->tkm/dot_general | solution.py:262
  164.2 4.6 %copy.111 = bf16[128,128,64]{0,2,1:T(8,128)(2,1)} copy(bf16[128,128,64]{1,2,0:T(8,128)(2,1)} %convolution_convert_fusion.4) | data formatting | bytes 4194304 | tf_op jit(solution)/shard_map/convert_element_type | solution.py:278
  168.8 7.9 %fusion.12 = f32[128,128,64]{1,2,0:T(8,128)} fusion(bf16[128,128,128]{2,1,0:T(8,128)(2,1)} %bitcast.93, bf16[128,128,64]{0,2,1:T(8,128)(2,1)} %copy.111), kind=kOutput, calls=%fused_computation.29 | convolution fusion | flops 268435456 | bytes 10485760 | tf_op jit(solution)/shard_map/tkm,kjm->tjk/dot_general | solution.py:262
  176.7 5.4 %copy.112 = f32[128,128,64]{0,2,1:T(8,128)} copy(f32[128,128,64]{1,2,0:T(8,128)} %fusion.12) | data formatting | bytes 8388608 | tf_op jit(solution)/shard_map/tkm,kjm->tjk/dot_general | solution.py:262
  182.1 4.2 %fusion.5 = bf16[64,128,128]{2,0,1:T(8,128)(2,1)S(1)} fusion(f32[128,128,64]{0,2,1:T(8,128)} %copy.112, bf16[128,128,64]{1,2,0:T(8,128)(2,1)} %get-tuple-element.67), kind=kLoop, calls=%fused_computation.6 | loop fusion | flops 11534336 | bytes 8388608 | tf_op jit(solution)/shard_map/convert_element_type | solution.py:282
  189.7 4.3 %convert_bitcast_fusion.1 = bf16[64,128,128]{1,0,2:T(8,128)(2,1)} fusion(bf16[128,128,128]{2,1,0:T(8,128)(2,1)S(1)} %bitcast.91, bf16[64,128,128]{2,0,1:T(8,128)(2,1)S(1)} %fusion.5), kind=kOutput, calls=%fused_computation.21 | convolution fusion | flops 269484032 | bytes 8388608 | tf_op jit(solution)/shard_map/tjk,jbk->tbj/dot_general | solution.py:262
  200.6 4.6 %copy.118 = bf16[64,128,128]{2,0,1:T(8,128)(2,1)} copy(bf16[64,128,128]{1,0,2:T(8,128)(2,1)} %convert_bitcast_fusion.1) | data formatting | bytes 4194304 | tf_op jit(solution)/shard_map/optimization_barrier | solution.py:285
  205.2 7.8 %all-to-all-start.2 = ((bf16[64,128,128]{2,0,1:T(8,128)(2,1)}), bf16[64,128,128]{2,0,1:T(8,128)(2,1)}, u32[]{:S(2)}, u32[]{:S(2)}) async-start(bf16[64,128,128]{2,0,1:T(8,128)(2,1)} %copy.118), calls=%async_computation.2 | async-start | bytes 4194304 | tf_op jit(solution)/shard_map/all_to_all | solution.py:253
  213.0 4.5 %copy.106 = bf16[64,128,128]{2,0,1:T(8,128)(2,1)} copy(bf16[64,128,128]{1,0,2:T(8,128)(2,1)} %convert_bitcast_fusion.2) | data formatting | bytes 4194304 | tf_op jit(solution)/shard_map/optimization_barrier | solution.py:275
  217.6 41.1 %all-to-all-done.2 = bf16[64,128,128]{2,0,1:T(8,128)(2,1)} async-done(((bf16[64,128,128]{2,0,1:T(8,128)(2,1)}), bf16[64,128,128]{2,0,1:T(8,128)(2,1)}, u32[]{:S(2)}, u32[]{:S(2)}) %all-to-all-start.2) | async-done | bytes 2097184 | tf_op jit(solution)/shard_map/all_to_all | solution.py:253
  258.6 7.8 %all-to-all-start.1 = ((bf16[64,128,128]{2,0,1:T(8,128)(2,1)}), bf16[64,128,128]{2,0,1:T(8,128)(2,1)}, u32[]{:S(2)}, u32[]{:S(2)}) async-start(bf16[64,128,128]{2,0,1:T(8,128)(2,1)} %copy.106), calls=%async_computation.1 | async-start | bytes 4194304 | tf_op jit(solution)/shard_map/all_to_all | solution.py:253
  273.0 90.3 %shard_map.110 = (f32[16,32,128]{2,1,0:T(8,128)S(1)}, f32[16,32,128]{2,1,0:T(8,128)S(1)}, f32[16,32,128]{2,1,0:T(8,128)S(1)}) custom-call(bf16[4,2,16,4,32,128]{5,4,3,2,1,0:T(8,128)(2,1)S(1)} %bitcast.87, bf16[4,2,16,4,32,128]{5,4,3,2,1,0:T(8,128)(2,1)S(1)} %bitcast.86, bf16[4,2,16,4,32,128]{5,4,3,2,1,0:T(8,128)(2,1)S(1)} %bitcast.85), custom_call_target="tpu_custom_call" | custom-call | bytes 67108864 | tf_op jit(solution)/shard_map/pallas_call | solution.py:221
  370.7 4.4 %all-to-all-start.3 = ((bf16[16,4,32,128]{3,2,0,1:T(8,128)(2,1)}), bf16[16,4,32,128]{3,2,0,1:T(8,128)(2,1)}, u32[]{:S(2)}, u32[]{:S(2)}) async-start(bf16[16,4,32,128]{3,2,0,1:T(8,128)(2,1)} %copy.122), calls=%async_computation.3 | async-start | bytes 1048576 | tf_op jit(solution)/shard_map/all_to_all | solution.py:291
  (46 shorter events, 47.8 us)
Async XLA Ops:
  0.6 3.1 copy-start
  98.6 50.6 %all-to-all-start = ((bf16[512,16,128]{2,1,0:T(8,128)(2,1)}), bf16[512,16,128]{2,1,0:T(8,128)(2,1)}, u32[]{:S(2)}, u32[]{:S(2)}) async-start(bf16[512,16,128]{2,1,0:T(8,128)(2,1)} %param.11), calls=%async_computation | async-start | bytes 4194304 | tf_op jit(solution)/shard_map/all_to_all | solution.py:249
  182.1 4.2 %copy-start.4 = (bf16[64,128,128]{1,0,2:T(8,128)(2,1)S(1)}, bf16[64,128,128]{1,0,2:T(8,128)(2,1)}, u32[]{:S(2)}) copy-start(bf16[64,128,128]{1,0,2:T(8,128)(2,1)} %copy.103) | copy-start | bytes 6291460
  186.3 3.4 copy-start.9
  189.7 4.3 %copy-start.5 = (bf16[128,128,64]{0,2,1:T(8,128)(2,1)S(1)}, bf16[128,128,64]{0,2,1:T(8,128)(2,1)}, u32[]{:S(2)}) copy-start(bf16[128,128,64]{0,2,1:T(8,128)(2,1)} %copy.111) | copy-start | bytes 6291460
  189.7 4.3 %copy-start.6 = (bf16[64,128,128]{1,0,2:T(8,128)(2,1)S(1)}, bf16[64,128,128]{1,0,2:T(8,128)(2,1)}, u32[]{:S(2)}) copy-start(bf16[64,128,128]{1,0,2:T(8,128)(2,1)} %copy.104) | copy-start | bytes 6291460
  194.0 3.3 copy-start.7
  194.0 3.3 copy-start.8
  205.2 53.4 %all-to-all-start.2 = ((bf16[64,128,128]{2,0,1:T(8,128)(2,1)}), bf16[64,128,128]{2,0,1:T(8,128)(2,1)}, u32[]{:S(2)}, u32[]{:S(2)}) async-start(bf16[64,128,128]{2,0,1:T(8,128)(2,1)} %copy.118), calls=%async_computation.2 | async-start | bytes 4194304 | tf_op jit(solution)/shard_map/all_to_all | solution.py:253
  258.6 112.0 %all-to-all-start.1 = ((bf16[64,128,128]{2,0,1:T(8,128)(2,1)}), bf16[64,128,128]{2,0,1:T(8,128)(2,1)}, u32[]{:S(2)}, u32[]{:S(2)}) async-start(bf16[64,128,128]{2,0,1:T(8,128)(2,1)} %copy.106), calls=%async_computation.1 | async-start | bytes 4194304 | tf_op jit(solution)/shard_map/all_to_all | solution.py:253
  266.5 2.2 copy-start.1
  268.7 2.2 copy-start.2
  270.9 2.2 copy-start.3
  363.4 2.2 copy-start.10
  370.7 12.2 %all-to-all-start.3 = ((bf16[16,4,32,128]{3,2,0,1:T(8,128)(2,1)}), bf16[16,4,32,128]{3,2,0,1:T(8,128)(2,1)}, u32[]{:S(2)}, u32[]{:S(2)}) async-start(bf16[16,4,32,128]{3,2,0,1:T(8,128)(2,1)} %copy.122), calls=%async_computation.3 | async-start | bytes 1048576 | tf_op jit(solution)/shard_map/all_to_all | solution.py:291
  378.6 1.6 copy-start.11

commit v3 on v2

--- a/solution.py
+++ b/solution.py
@@ -75,8 +75,8 @@
         ])
     for f in range(count):
         own[f].start()
-        for copy in stage_z[f]:
-            copy.start()
+    for copy in stage_z[0]:
+        copy.start()
 
     def spread(f, stage, lo_part, hi_part):
         copies = [
@@ -93,6 +93,9 @@
         own[f].wait()
         for copy in stage_z[f]:
             copy.wait()
+        if f + 1 < count:
+            for copy in stage_z[f + 1]:
+                copy.start()
         first.append(spread(f, 0, wholes[f].at[:, c, hi, lo, 0], wholes[f].at[:, c, hi, lo, 1]))
     keep.start()
     for copy in swaps:
@@ -162,12 +165,14 @@
     for f in range(count):
         stage_c.append(remote(grads[f].at[:, 1 - c], got_c.at[f], cs.at[f], cr.at[f], sibling))
         local.append(pltpu.make_async_copy(grads[f].at[:, c], own.at[f], own_sem.at[f]))
-        stage_c[f].start()
         local[f].start()
+    stage_c[0].start()
     stage_d = []
     for f in range(count):
         stage_c[f].wait()
         local[f].wait()
+        if f + 1 < count:
+            stage_c[f + 1].start()
 
         def core_sum(k, carry):
             for q in range(n_dp):
@@ -274,7 +279,6 @@
         w2 = dot("tkm,mkn->tnm", u2, left_two).astype(bf)
         dw_two, w2 = lax.optimization_barrier((dw_two, w2))
         mixed = to_blocks(w2)
-        layer_out = (tokens_in.astype(f32) + mixed.astype(f32)).astype(bf)
         du2 = dot("tnm,mkn->tkm", dw_two, left_two).astype(bf)
         gl2 = dot("tkm,tnm->mkn", u2, dw_two)
         gr2 = dot("tjk,tkm->kjm", hidden, du2)
@@ -282,9 +286,12 @@
         dz1 = (dh * gelu_slope(z1.astype(f32))).astype(bf)
         dv1 = dot("tjk,jbk->tbj", dz1, left_one).astype(bf)
         gl1 = dot("tbj,tjk->jbk", v1, dz1)
-        dv1, gl2, gr2, gl1 = lax.optimization_barrier((dv1, gl2.astype(bf), gr2.astype(bf), gl1.astype(bf)))
+        mixed, dv1, gl2, gr2, gl1 = lax.optimization_barrier(
+            (mixed, dv1, gl2.astype(bf), gr2.astype(bf), gl1.astype(bf))
+        )
         du1 = to_blocks(dv1)
         gl2, gr2, gl1 = reduce_all((gl2, gr2, gl1), n_dp, n_z)
+        layer_out = (tokens_in.astype(f32) + mixed.astype(f32)).astype(bf)
         gr1 = dot("tbi,tbo->bio", tokens_in, du1)
         input_grad = (out_grad.astype(f32) + dot("tbo,bio->tbi", du1, right_one)).astype(bf)
         gr1 = gr1.astype(bf).reshape(gr1.shape[0], n_dp, -1, gr1.shape[2])

time: 388 us -> 350 us (0.902)
  waiting for transfers between devices: 57.5 us -> 18.4 us
    all_to_all x2, waiting for transfers between devices: 41.1 us -> 0.01 us  [to_blocks(): lax.all_to_all(values, 'tensor', split_axis=1, concat_axis=0, tiled=True)]
    unnamed x29 -> x33, local copies, waits for them, and re-layouts: 15.9 us -> 15.1 us
  transfers between devices with their start and end apart: 4 -> 4, of which waited for: 3 -> 2; matrix products, arithmetic and copies ran while one was open for 12% -> 24% of each run, Pallas kernels for 23% -> 26%
where the time goes in v3:
time: 350 us; the launch traced here: 348 us
  Pallas kernels  176 us (50%)
  local copies, waits for them, and re-layouts  70 us (20%)
  matrix products  51.1 us (15%)
  starting transfers between devices  24.3 us (7%)
  waiting for transfers between devices  18.4 us (5%)
  other arithmetic  7.65 us (2%)
    pallas_call x1, Pallas kernels, reduce_all(): pl.pallas_call(lambda *refs: reduce_kernel(n_dp, n_z, count, *refs), out_...  91.3 us
    pallas_call x1, Pallas kernels, gather_and_swap(): pl.pallas_call(lambda *refs: gather_kernel(n_dp, n_z, count, *refs), out_...  85 us
    dot_general x12, matrix products, dot(): return jnp.einsum(spec, a, b, preferred_element_type=f32)  51.1 us
    all_to_all x1, waiting for transfers between devices, to_tokens(): lax.all_to_all(values, 'tensor', split_axis=0, concat_axis=1, tiled=True)  15.5 us
    unnamed x33, local copies, waits for them, and re-layouts  15.1 us
    all_to_all x2, starting transfers between devices, to_blocks(): lax.all_to_all(values, 'tensor', split_axis=1, concat_axis=0, tiled=True)  14 us
    optimization_barrier x2, local copies, waits for them, and re-layouts, on_device(): dw_two, w2 = lax.optimization_barrier((dw_two, w2))  8.65 us
  transfers between devices with their start and end apart: 4, of which 2 were waited for; matrix products, arithmetic and copies ran while one was open for 24% of the time, Pallas kernels for 26%

profile of v3, /device:TPU:8, one launch (start us, length us, event | category | flops | bytes accessed | tf_op | source)
XLA Modules:
  0.0 348.5 jit_solution(4167437633497460926)
XLA Ops:
  5.8 4.5 %copy.100 = bf16[512,16,128]{2,1,0:T(8,128)(2,1)} copy(bf16[512,16,128]{0,2,1:T(8,128)(2,1)} %convert_bitcast_fusion.3) | data formatting | bytes 4194304 | tf_op jit(solution)/shard_map/convert_element_type | solution.py:269
  10.3 85.0 %shard_map.109 = (bf16[4,2,2,2,2,256,128]{6,5,4,3,2,1,0:T(8,128)(2,1)}, bf16[4,2,2,2,2,256,128]{6,5,4,3,2,1,0:T(8,128)(2,1)}, bf16[4,2,2,2,2,256,128]{6,5,4,3,2,1,0:T(8,128)(2,1)}, bf16[8,64,16,128]{3,2,1,0:T(8,128)(2,1)}) custom-call(bf16[4,2,256,128]{3,2,1,0:T(8,128)(2,1)} %bitcast.98, bf16[4,2,256,128]{3,2,1,0:T(8,128)(2,1)} %bitcast.99, ...), custom_call_target="tpu_custom_call" | custom-call | bytes 67108864 | tf_op jit(solution)/shard_map/pallas_call | solution.py:131
  98.9 6.1 %all-to-all-start = ((bf16[512,16,128]{2,1,0:T(8,128)(2,1)}), bf16[512,16,128]{2,1,0:T(8,128)(2,1)}, u32[]{:S(2)}, u32[]{:S(2)}) async-start(bf16[512,16,128]{2,1,0:T(8,128)(2,1)} %param.11), calls=%async_computation | async-start | bytes 4194304 | tf_op jit(solution)/shard_map/all_to_all | solution.py:254
  105.0 4.1 %copy.103 = bf16[64,128,128]{1,0,2:T(8,128)(2,1)} copy(bf16[64,128,128]{2,1,0:T(8,128)(2,1)} %bitcast.95) | data formatting | bytes 4194304 | tf_op jit(solution)/shard_map/optimization_barrier | solution.py:274
  109.1 6.1 %fusion.8 = (bf16[64,128,128]{2,0,1:T(8,128)(2,1)}, bf16[128,128,64]{1,2,0:T(8,128)(2,1)}) fusion(bf16[64,128,128]{1,0,2:T(8,128)(2,1)} %copy.103, bf16[128,128,128]{2,1,0:T(8,128)(2,1)} %bitcast.86), kind=kOutput, calls=%fused_computation.12 | convolution fusion | flops 275775488 | bytes 10485760 | tf_op jit(solution)/shard_map/tbj,jbk->tjk/dot_general | solution.py:267
  115.1 4.6 %copy.104 = bf16[64,128,128]{1,0,2:T(8,128)(2,1)} copy(bf16[64,128,128]{2,0,1:T(8,128)(2,1)} %get-tuple-element.68) | data formatting | bytes 4194304 | tf_op jit(solution)/shard_map/convert_element_type | solution.py:277
  119.7 5.4 %convert_bitcast_fusion.2 = bf16[64,128,128]{2,0,1:T(8,128)(2,1)} fusion(bf16[64,128,128]{1,0,2:T(8,128)(2,1)} %copy.104, bf16[128,128,128]{2,1,0:T(8,128)(2,1)} %bitcast.88), kind=kOutput, calls=%fused_computation.21 | convolution fusion | flops 269484032 | bytes 8388608 | tf_op jit(solution)/shard_map/tjk,kjm->tkm/dot_general | solution.py:267
  125.1 4.6 %copy.105 = bf16[64,128,128]{1,0,2:T(8,128)(2,1)} copy(bf16[64,128,128]{2,0,1:T(8,128)(2,1)} %convert_bitcast_fusion.2) | data formatting | bytes 4194304 | tf_op jit(solution)/shard_map/convert_element_type | solution.py:278
  129.7 5.4 %convert_bitcast_fusion.1 = bf16[64,128,128]{1,0,2:T(8,128)(2,1)} fusion(bf16[64,128,128]{1,0,2:T(8,128)(2,1)} %copy.105, bf16[128,128,128]{2,1,0:T(8,128)(2,1)} %bitcast.90), kind=kOutput, calls=%fused_computation.20 | convolution fusion | flops 269484032 | bytes 8388608 | tf_op jit(solution)/shard_map/tkm,mkn->tnm/dot_general | solution.py:267
  135.1 15.5 %all-to-all-done = bf16[512,16,128]{2,1,0:T(8,128)(2,1)} async-done(((bf16[512,16,128]{2,1,0:T(8,128)(2,1)}), bf16[512,16,128]{2,1,0:T(8,128)(2,1)}, u32[]{:S(2)}, u32[]{:S(2)}) %all-to-all-start) | async-done | bytes 2097184 | tf_op jit(solution)/shard_map/all_to_all | solution.py:254
  154.1 4.5 %copy.106 = bf16[64,128,128]{2,0,1:T(8,128)(2,1)} copy(bf16[64,128,128]{1,0,2:T(8,128)(2,1)} %convert_bitcast_fusion.1) | data formatting | bytes 4194304 | tf_op jit(solution)/shard_map/optimization_barrier | solution.py:280
  158.7 7.8 %all-to-all-start.1 = ((bf16[64,128,128]{2,0,1:T(8,128)(2,1)}), bf16[64,128,128]{2,0,1:T(8,128)(2,1)}, u32[]{:S(2)}, u32[]{:S(2)}) async-start(bf16[64,128,128]{2,0,1:T(8,128)(2,1)} %copy.106), calls=%async_computation.1 | async-start | bytes 4194304 | tf_op jit(solution)/shard_map/all_to_all | solution.py:258
  166.5 4.1 %copy.109 = bf16[64,128,128]{1,0,2:T(8,128)(2,1)} copy(bf16[64,128,128]{2,1,0:T(8,128)(2,1)} %bitcast.94) | data formatting | bytes 4194304 | tf_op jit(solution)/shard_map/optimization_barrier | solution.py:280
  170.6 7.2 %convolution_convert_fusion.4 = bf16[128,128,64]{1,2,0:T(8,128)(2,1)} fusion(bf16[128,128,128]{2,1,0:T(8,128)(2,1)} %bitcast.91, bf16[64,128,128]{1,0,2:T(8,128)(2,1)} %copy.109), kind=kOutput, calls=%fused_computation.24 | convolution fusion | flops 269484032 | bytes 8388608 | tf_op jit(solution)/shard_map/tnm,mkn->tkm/dot_general | solution.py:267
  177.8 4.6 %copy.110 = bf16[128,128,64]{0,2,1:T(8,128)(2,1)} copy(bf16[128,128,64]{1,2,0:T(8,128)(2,1)} %convolution_convert_fusion.4) | data formatting | bytes 4194304 | tf_op jit(solution)/shard_map/convert_element_type | solution.py:282
  182.4 7.8 %fusion.11 = f32[128,128,64]{1,2,0:T(8,128)} fusion(bf16[128,128,128]{2,1,0:T(8,128)(2,1)} %bitcast.89, bf16[128,128,64]{0,2,1:T(8,128)(2,1)} %copy.110), kind=kOutput, calls=%fused_computation.27 | convolution fusion | flops 268435456 | bytes 10485760 | tf_op jit(solution)/shard_map/tkm,kjm->tjk/dot_general | solution.py:267
  190.2 5.5 %copy.111 = f32[128,128,64]{0,2,1:T(8,128)} copy(f32[128,128,64]{1,2,0:T(8,128)} %fusion.11) | data formatting | bytes 8388608 | tf_op jit(solution)/shard_map/tkm,kjm->tjk/dot_general | solution.py:267
  195.7 3.9 %fusion.5 = bf16[64,128,128]{2,0,1:T(8,128)(2,1)S(1)} fusion(f32[128,128,64]{0,2,1:T(8,128)} %copy.111, bf16[128,128,64]{1,2,0:T(8,128)(2,1)} %get-tuple-element.69), kind=kLoop, calls=%fused_computation.6 | loop fusion | flops 11534336 | bytes 8388608 | tf_op jit(solution)/shard_map/convert_element_type | solution.py:286
  202.9 4.3 %convert_bitcast_fusion = bf16[64,128,128]{1,0,2:T(8,128)(2,1)} fusion(bf16[128,128,128]{2,1,0:T(8,128)(2,1)S(1)} %bitcast.87, bf16[64,128,128]{2,0,1:T(8,128)(2,1)S(1)} %fusion.5), kind=kOutput, calls=%fused_computation.19 | convolution fusion | flops 269484032 | bytes 8388608 | tf_op jit(solution)/shard_map/tjk,jbk->tbj/dot_general | solution.py:267
  213.8 4.3 %copy.108 = bf16[8,64,16,128]{3,2,1,0:T(8,128)(2,1)} copy(bf16[8,64,16,128]{3,1,2,0:T(8,128)(2,1)} %bitcast.18) | data formatting | bytes 4194304 | tf_op jit(solution)/shard_map/all_to_all | solution.py:258
  218.1 4.6 %copy.118 = bf16[64,128,128]{2,0,1:T(8,128)(2,1)} copy(bf16[64,128,128]{1,0,2:T(8,128)(2,1)} %convert_bitcast_fusion) | data formatting | bytes 4194304 | tf_op jit(solution)/shard_map/optimization_barrier | solution.py:289
  222.7 6.2 %all-to-all-start.2 = ((bf16[64,128,128]{2,0,1:T(8,128)(2,1)}), bf16[64,128,128]{2,0,1:T(8,128)(2,1)}, u32[]{:S(2)}, u32[]{:S(2)}) async-start(bf16[64,128,128]{2,0,1:T(8,128)(2,1)} %copy.118), calls=%async_computation.2 | async-start | bytes 4194304 | tf_op jit(solution)/shard_map/all_to_all | solution.py:258
  235.4 91.3 %shard_map.110 = (f32[16,32,128]{2,1,0:T(8,128)S(1)}, f32[16,32,128]{2,1,0:T(8,128)S(1)}, f32[16,32,128]{2,1,0:T(8,128)S(1)}) custom-call(bf16[4,2,16,4,32,128]{5,4,3,2,1,0:T(8,128)(2,1)S(1)} %bitcast.83, bf16[4,2,16,4,32,128]{5,4,3,2,1,0:T(8,128)(2,1)S(1)} %bitcast.82, bf16[4,2,16,4,32,128]{5,4,3,2,1,0:T(8,128)(2,1)S(1)} %bitcast.81), custom_call_target="tpu_custom_call" | custom-call | bytes 67108864 | tf_op jit(solution)/shard_map/pallas_call | solution.py:226
  332.5 4.1 %all-to-all-start.3 = ((bf16[16,4,32,128]{3,2,0,1:T(8,128)(2,1)}), bf16[16,4,32,128]{3,2,0,1:T(8,128)(2,1)}, u32[]{:S(2)}, u32[]{:S(2)}) async-start(bf16[16,4,32,128]{3,2,0,1:T(8,128)(2,1)} %copy.122), calls=%async_computation.3 | async-start | bytes 1048576 | tf_op jit(solution)/shard_map/all_to_all | solution.py:298
  (48 shorter events, 46.3 us)
Async XLA Ops:
  0.6 3.1 copy-start
  98.9 51.7 %all-to-all-start = ((bf16[512,16,128]{2,1,0:T(8,128)(2,1)}), bf16[512,16,128]{2,1,0:T(8,128)(2,1)}, u32[]{:S(2)}, u32[]{:S(2)}) async-start(bf16[512,16,128]{2,1,0:T(8,128)(2,1)} %param.11), calls=%async_computation | async-start | bytes 4194304 | tf_op jit(solution)/shard_map/all_to_all | solution.py:254
  158.7 55.1 %all-to-all-start.1 = ((bf16[64,128,128]{2,0,1:T(8,128)(2,1)}), bf16[64,128,128]{2,0,1:T(8,128)(2,1)}, u32[]{:S(2)}, u32[]{:S(2)}) async-start(bf16[64,128,128]{2,0,1:T(8,128)(2,1)} %copy.106), calls=%async_computation.1 | async-start | bytes 4194304 | tf_op jit(solution)/shard_map/all_to_all | solution.py:258
  195.7 4.0 %copy-start.4 = (bf16[64,128,128]{1,0,2:T(8,128)(2,1)S(1)}, bf16[64,128,128]{1,0,2:T(8,128)(2,1)}, u32[]{:S(2)}) copy-start(bf16[64,128,128]{1,0,2:T(8,128)(2,1)} %copy.103) | copy-start | bytes 6291460
  199.7 3.3 copy-start.10
  202.9 4.3 %copy-start.5 = (bf16[128,128,64]{0,2,1:T(8,128)(2,1)S(1)}, bf16[128,128,64]{0,2,1:T(8,128)(2,1)}, u32[]{:S(2)}) copy-start(bf16[128,128,64]{0,2,1:T(8,128)(2,1)} %copy.110) | copy-start | bytes 6291460
  202.9 4.3 %copy-start.7 = (bf16[64,128,128]{1,0,2:T(8,128)(2,1)S(1)}, bf16[64,128,128]{1,0,2:T(8,128)(2,1)}, u32[]{:S(2)}) copy-start(bf16[64,128,128]{1,0,2:T(8,128)(2,1)} %copy.104) | copy-start | bytes 6291460
  207.2 3.3 copy-start.8
  207.2 3.3 copy-start.9
  222.7 105.9 %all-to-all-start.2 = ((bf16[64,128,128]{2,0,1:T(8,128)(2,1)}), bf16[64,128,128]{2,0,1:T(8,128)(2,1)}, u32[]{:S(2)}, u32[]{:S(2)}) async-start(bf16[64,128,128]{2,0,1:T(8,128)(2,1)} %copy.118), calls=%async_computation.2 | async-start | bytes 4194304 | tf_op jit(solution)/shard_map/all_to_all | solution.py:258
  228.8 2.2 copy-start.1
  231.0 2.2 copy-start.2
  233.2 2.2 copy-start.3
  235.4 91.3 %copy-start.11 = (bf16[512,16,128]{2,1,0:T(8,128)(2,1)S(1)}, bf16[512,16,128]{2,1,0:T(8,128)(2,1)}, u32[]{:S(2)}) copy-start(bf16[512,16,128]{2,1,0:T(8,128)(2,1)} %param.6) | copy-start | bytes 6291460
  235.4 91.3 %copy-start.12 = (bf16[8,64,16,128]{3,2,1,0:T(8,128)(2,1)S(1)}, bf16[8,64,16,128]{3,2,1,0:T(8,128)(2,1)}, u32[]{:S(2)}) copy-start(bf16[8,64,16,128]{3,2,1,0:T(8,128)(2,1)} %copy.108) | copy-start | bytes 6291460
  330.3 1.3 copy-start.6
  331.6 5.0 %copy-start.13 = (bf16[512,16,128]{2,1,0:T(8,128)(2,1)S(1)}, bf16[512,16,128]{2,1,0:T(8,128)(2,1)}, u32[]{:S(2)}) copy-start(bf16[512,16,128]{2,1,0:T(8,128)(2,1)} %param.11) | copy-start | bytes 6291460
  332.5 12.1 %all-to-all-start.3 = ((bf16[16,4,32,128]{3,2,0,1:T(8,128)(2,1)}), bf16[16,4,32,128]{3,2,0,1:T(8,128)(2,1)}, u32[]{:S(2)}, u32[]{:S(2)}) async-start(bf16[16,4,32,128]{3,2,0,1:T(8,128)(2,1)} %copy.122), calls=%async_computation.3 | async-start | bytes 1048576 | tf_op jit(solution)/shard_map/all_to_all | solution.py:298
